TPU v7x, 512 devices: a whole 4x4x16 slice. The times are simulated.
512 devices in a mesh: row: 8 (over x, core), col: 64 (over y, z).
Axes of the slice: x: 4, y: 4, z: 16, core: 2. Of those that a mesh axis runs over, the one named last changes fastest.
Arguments:
- teacher_tokens: bfloat16 [512, 8192], P('col', 'row'), may hold values from -6 to 6
- student_tokens: bfloat16 [512, 8192], P('col', 'row'), may hold values from -6 to 6
- gate_weight: bfloat16 [8192, 29568], P('row', 'col'), may hold values from -0.0625 to 0.0625
- up_weight: bfloat16 [8192, 29568], P('row', 'col'), may hold values from -0.0625 to 0.0625
- down_weight: bfloat16 [29568, 8192], P('col', 'row'), may hold values from -0.03125 to 0.03125
- expert_ids: int32 [512, 6], P('col'), may hold values from 0 to 63, as said below
- slot_ids: int32 [512, 6], P('col'), may hold values from 0 to 1, as said below
- route_weights: bfloat16 [512, 6], P('col'), may hold values from 1 to 8
Outputs:
- teacher_out: bfloat16 [512, 8192], P('col', 'row')
- student_out: bfloat16 [512, 8192], P('col', 'row')
- input_grad: bfloat16 [512, 8192], P('col', 'row')
Inputs may be any that keep to these rules, and one draw needn't show every extreme that they name: `expert_ids`: each token names 6 different experts. Among the 8 tokens of one block no expert is named more than 2 times, and some expert is named exactly 2 times by every block. `slot_ids`: within one block of 8 tokens the choices of one expert carry different slots.
All inputs are finite; a program needn't handle non-finite values.
Results may differ from a plain program's by a relative error of at most 0.01.
Values may be sent and summed in bfloat16 or wider, within the bound.
A program may use at most 64 MiB of HBM per device.

v0:
```python
import jax
import jax.numpy as jnp
from jax import lax
from jax.sharding import PartitionSpec as P

EXP_DEV = 1


def silu_slope(value):
    logistic = jax.nn.sigmoid(value)
    return logistic * (1.0 + value * (1.0 - logistic))


def to_experts(flat, col_count, capacity):
    width = flat.shape[1]
    return (
        flat.reshape(col_count, EXP_DEV, capacity, width)
        .transpose(1, 0, 2, 3)
        .reshape(EXP_DEV, col_count * capacity, width)
    )


def from_experts(grouped, col_count, capacity):
    width = grouped.shape[2]
    return (
        grouped.reshape(EXP_DEV, col_count, capacity, width)
        .transpose(1, 0, 2, 3)
        .reshape(col_count * EXP_DEV * capacity, width)
    )


def shards(
    teacher_tokens,
    student_tokens,
    gate_weight,
    up_weight,
    down_weight,
    expert_ids,
    slot_ids,
    route_weights,
):
    col_count = lax.axis_size("col")
    token_rows = teacher_tokens.shape[0]
    width_rows = teacher_tokens.shape[1]
    unit_count = gate_weight.shape[1]
    hidden_units = unit_count // EXP_DEV
    top_count = expert_ids.shape[1]
    capacity = max(2, token_rows * top_count // (EXP_DEV * col_count) * 2)
    owned_slots = EXP_DEV * capacity
    slots_all = col_count * owned_slots
    target = expert_ids * capacity + slot_ids
    slot_range = jnp.arange(slots_all, dtype=jnp.int32)
    matches = target[:, :, None] == slot_range[None, None, :]
    placing = jnp.sum(matches, axis=1).astype(jnp.bfloat16)
    weighting = jnp.sum(
        jnp.where(matches, route_weights[:, :, None].astype(jnp.float32), 0.0), axis=1
    ).astype(jnp.bfloat16)
    teacher_all = lax.all_gather(teacher_tokens, "col", axis=0, tiled=True)
    outgoing = jnp.einsum(
        "tq,td->qd", placing, student_tokens, preferred_element_type=jnp.float32
    ).astype(jnp.bfloat16)
    arrived = lax.all_to_all(outgoing, "col", split_axis=0, concat_axis=0, tiled=True)
    gate_part = jnp.dot(teacher_all, gate_weight, preferred_element_type=jnp.float32)
    up_part = jnp.dot(teacher_all, up_weight, preferred_element_type=jnp.float32)
    gate_sum, up_sum = lax.psum((gate_part, up_part), "row")
    hidden = (jax.nn.silu(gate_sum) * up_sum).astype(jnp.bfloat16)
    teacher_out = lax.psum_scatter(
        jnp.dot(hidden, down_weight, preferred_element_type=jnp.float32),
        "col",
        scatter_dimension=0,
        tiled=True,
    ).astype(jnp.bfloat16)
    gate_blocks = gate_weight.reshape(width_rows, EXP_DEV, hidden_units)
    up_blocks = up_weight.reshape(width_rows, EXP_DEV, hidden_units)
    down_blocks = down_weight.reshape(EXP_DEV, hidden_units, width_rows)
    by_expert = to_experts(arrived, col_count, capacity)
    gate_local = jnp.einsum(
        "esd,deh->esh", by_expert, gate_blocks, preferred_element_type=jnp.float32
    )
    up_local = jnp.einsum("esd,deh->esh", by_expert, up_blocks, preferred_element_type=jnp.float32)
    pre_gate, pre_up = lax.psum((gate_local, up_local), "row")
    activated = (jax.nn.silu(pre_gate) * pre_up).astype(jnp.bfloat16)
    produced = jnp.einsum(
        "esh,ehd->esd", activated, down_blocks, preferred_element_type=jnp.float32
    ).astype(jnp.bfloat16)
    returned = lax.all_to_all(
        from_experts(produced, col_count, capacity), "col", split_axis=0, concat_axis=0, tiled=True
    )
    student_out = jnp.dot(weighting, returned, preferred_element_type=jnp.float32).astype(
        jnp.bfloat16
    )
    loss_grad = (student_out.astype(jnp.float32) - teacher_out.astype(jnp.float32)).astype(
        jnp.bfloat16
    )
    grad_out = jnp.einsum(
        "tq,td->qd", weighting, loss_grad, preferred_element_type=jnp.float32
    ).astype(jnp.bfloat16)
    grad_arrived = lax.all_to_all(grad_out, "col", split_axis=0, concat_axis=0, tiled=True)
    grad_by_expert = to_experts(grad_arrived, col_count, capacity)
    hidden_local = jnp.einsum(
        "esd,ehd->esh", grad_by_expert, down_blocks, preferred_element_type=jnp.float32
    )
    hidden_grad = lax.psum(hidden_local, "row")
    gate_grad = (hidden_grad * pre_up * silu_slope(pre_gate)).astype(jnp.bfloat16)
    up_grad = (hidden_grad * jax.nn.silu(pre_gate)).astype(jnp.bfloat16)
    row_grad = jnp.einsum(
        "esh,deh->esd", gate_grad, gate_blocks, preferred_element_type=jnp.float32
    )
    row_grad = row_grad + jnp.einsum(
        "esh,deh->esd", up_grad, up_blocks, preferred_element_type=jnp.float32
    )
    row_grad = row_grad.astype(jnp.bfloat16)
    back_rows = lax.all_to_all(
        from_experts(row_grad, col_count, capacity), "col", split_axis=0, concat_axis=0, tiled=True
    )
    input_grad = jnp.dot(placing, back_rows, preferred_element_type=jnp.float32).astype(
        jnp.bfloat16
    )
    return (teacher_out, student_out, input_grad)


def solution(mesh):
    return jax.shard_map(
        shards,
        mesh=mesh,
        in_specs=(
            P("col", "row"),
            P("col", "row"),
            P("row", "col"),
            P("row", "col"),
            P("col", "row"),
            P("col", None),
            P("col", None),
            P("col", None),
        ),
        out_specs=(P("col", "row"), P("col", "row"), P("col", "row")),
        check_vma=False,
    )
```

profile of v0, /device:TPU:1, one launch (start us, length us, event | category | flops | bytes accessed | tf_op | source)
XLA Modules:
  0.0 1076.2 jit_solution(6106732638161341930)
XLA Ops:
  7.2 0.7 all-gather.2.cloned.1.call-update
  8.0 0.7 multiply_add_fusion
  8.9 1.0 convolution_convert_fusion.2
  9.9 38.3 %all_to_all.42 = bf16[64,2,1024]{2,1,0:T(2,128)(2,1)S(1)} all-to-all(bf16[64,2,1024]{2,1,0:T(2,128)(2,1)S(1)} %all_to_all.28), channel_id=1, replica_groups=mesh['row'=8,'col'=64] {'col'}, dimensions={0} | all-to-all | bytes 524288 | tf_op jit(solution)/shard_map/all_to_all | solution.py:62
  48.4 1.1 convolution_bitcast_fusion.1
  49.5 1.1 convolution_bitcast_fusion.2
  50.6 95.6 %all-gather.2.cloned.1.call-done = bf16[512,1024]{1,0:T(8,128)(2,1)} async-done(((bf16[8,1024]{1,0:T(8,128)(2,1)}), bf16[512,1024]{1,0:T(8,128)(2,1)}) %all-gather.2.cloned.1.call-update) | async-done | bytes 1048592 | tf_op jit(solution)/shard_map/all_gather | solution.py:58
  146.1 3.0 fusion.21
  149.1 1.7 fusion.20
  150.8 86.3 %all-reduce.6.cloned.1.call-done = (f32[512,462]{0,1:T(8,128)}, f32[512,462]{0,1:T(8,128)}, f32[1,128,462]{1,2,0:T(8,128)}, f32[1,128,462]{1,2,0:T(8,128)}) async-done(((f32[512,462]{0,1:T(8,128)}, f32[512,462]{0,1:T(8,128)}, f32[1,128,462]{1,2,0:T(8,128)}, f32[1,128,462]{1,2,0:T(8,128)}), (f32[512,462]{0,1:T(8,128)}, f32[512,462]{0,1:T(8,128)}, f32[1,128,462]{1,2,0:T(8,128)}, ...) | async-done | bytes 2365456 | tf_op jit(solution)/shard_map/psum | solution.py:65
  237.1 3.6 fusion.1
  240.6 0.9 copy-done.3
  241.6 1.3 convolution_convert_fusion.1
  242.9 0.8 all_to_all.30
  243.7 15.0 %all-to-all-start.1 = ((bf16[64,2,1024]{2,1,0:T(2,128)(2,1)}), bf16[64,2,1024]{2,1,0:T(2,128)(2,1)S(1)}, u32[]{:S(2)}, u32[]{:S(2)}) async-start(bf16[64,2,1024]{2,1,0:T(2,128)(2,1)} %all_to_all.30), calls=%async_computation.2 | async-start | bytes 524288 | tf_op jit(solution)/shard_map/all_to_all | solution.py:86
  258.9 17.2 %all-to-all-done.1 = bf16[64,2,1024]{2,1,0:T(2,128)(2,1)S(1)} async-done(((bf16[64,2,1024]{2,1,0:T(2,128)(2,1)}), bf16[64,2,1024]{2,1,0:T(2,128)(2,1)S(1)}, u32[]{:S(2)}, u32[]{:S(2)}) %all-to-all-start.1) | async-done | bytes 262176 | tf_op jit(solution)/shard_map/all_to_all | solution.py:86
  276.4 651.2 %reduce-scatter.2.cloned.1.call-done = f32[8,1024]{1,0:T(8,128)} async-done(((f32[512,1024]{1,0:T(8,128)}), f32[8,1024]{1,0:T(8,128)}) %reduce-scatter.2.cloned.1.call-update) | async-done | bytes 32784 | tf_op jit(solution)/shard_map/reduce_scatter | solution.py:67
  927.6 0.8 convert_element_type.58
  928.7 26.0 %all_to_all.43 = bf16[64,2,1024]{2,1,0:T(2,128)(2,1)S(1)} all-to-all(bf16[64,2,1024]{2,1,0:T(2,128)(2,1)S(1)} %all_to_all.33), channel_id=1, replica_groups=mesh['row'=8,'col'=64] {'col'}, dimensions={0} | all-to-all | bytes 524288 | tf_op jit(solution)/shard_map/all_to_all | solution.py:98
  954.8 1.1 convolution_bitcast_fusion
  956.0 79.5 %all-reduce.4.cloned.1.call-done = f32[1,128,462]{1,2,0:T(8,128)} async-done(((f32[1,128,462]{1,2,0:T(8,128)}), f32[1,128,462]{1,2,0:T(8,128)}) %all-reduce.4.cloned.1.call-update) | async-done | bytes 236560 | tf_op jit(solution)/shard_map/psum | solution.py:103
  1035.5 1.6 fusion.8
  1037.6 31.2 %all_to_all.44 = bf16[64,2,1024]{2,1,0:T(2,128)(2,1)S(1)} all-to-all(bf16[64,2,1024]{2,1,0:T(2,128)(2,1)S(1)} %all_to_all.35), channel_id=1, replica_groups=mesh['row'=8,'col'=64] {'col'}, dimensions={0} | all-to-all | bytes 524288 | tf_op jit(solution)/shard_map/all_to_all | solution.py:113
  1069.0 0.8 convolution_convert_fusion.3
  (40 shorter events, 2.1 us)
Async XLA Ops:
  7.2 229.9 %copy-start = (bf16[462,1024]{1,0:T(8,128)(2,1)S(1)}, bf16[462,1024]{1,0:T(8,128)(2,1)}, u32[]{:S(2)}) copy-start(bf16[462,1024]{1,0:T(8,128)(2,1)} %param.12) | copy-start | bytes 2838532
  7.2 41.2 %copy-start.2 = (bf16[1024,462]{0,1:T(8,128)(2,1)S(1)}, bf16[1024,462]{0,1:T(8,128)(2,1)}, u32[]{:S(2)}) copy-start(bf16[1024,462]{0,1:T(8,128)(2,1)} %param.11) | copy-start | bytes 2838532
  7.2 42.3 %copy-start.1 = (bf16[1024,462]{0,1:T(8,128)(2,1)S(1)}, bf16[1024,462]{0,1:T(8,128)(2,1)}, u32[]{:S(2)}) copy-start(bf16[1024,462]{0,1:T(8,128)(2,1)} %param.10) | copy-start | bytes 2838532
  7.2 138.9 %all-gather.2.cloned.1.call-start = ((), (), s32[]{:S(2)}) async-start(), calls=%async_computation.5 | async-start | bytes 1064960 | tf_op jit(solution)/shard_map/all_gather | solution.py:58
  7.9 229.1 %all-reduce.6.cloned.1.call-start = ((), (), s32[]{:S(2)}) async-start(), calls=%async_computation.8 | async-start | bytes 4751360 | tf_op jit(solution)/shard_map/psum | solution.py:65
  146.1 3.0 copy-start.9
  150.8 776.8 %reduce-scatter.2.cloned.1.call-start = ((), (), s32[]{:S(2)}) async-start(), calls=%async_computation.6 | async-start | bytes 2129920 | tf_op jit(solution)/shard_map/reduce_scatter | solution.py:67
  240.6 0.9 copy-start.3
  240.6 18.1 %copy-start.8 = (bf16[8,6]{1,0:T(8,128)(2,1)S(1)}, bf16[8,6]{1,0:T(8,128)(2,1)}, u32[]{:S(2)}) copy-start(bf16[8,6]{1,0:T(8,128)(2,1)} %param.15) | copy-start | bytes 292
  243.7 32.5 %all-to-all-start.1 = ((bf16[64,2,1024]{2,1,0:T(2,128)(2,1)}), bf16[64,2,1024]{2,1,0:T(2,128)(2,1)S(1)}, u32[]{:S(2)}, u32[]{:S(2)}) async-start(bf16[64,2,1024]{2,1,0:T(2,128)(2,1)} %all_to_all.30), calls=%async_computation.2 | async-start | bytes 524288 | tf_op jit(solution)/shard_map/all_to_all | solution.py:86
  258.7 776.8 %all-reduce.4.cloned.1.call-start = ((), (), s32[]{:S(2)}) async-start(), calls=%async_computation.7 | async-start | bytes 475136 | tf_op jit(solution)/shard_map/psum | solution.py:103
  276.4 760.7 %copy-start.6 = (bf16[8,1024]{1,0:T(8,128)(2,1)}, bf16[8,1024]{1,0:T(8,128)(2,1)S(1)}, u32[]{:S(2)}) copy-start(bf16[8,1024]{1,0:T(8,128)(2,1)S(1)} %convolution_convert_fusion.4) | copy-start | bytes 49156
  928.4 108.8 %copy-start.7 = (bf16[8,1024]{1,0:T(8,128)(2,1)}, bf16[8,1024]{1,0:T(8,128)(2,1)S(1)}, u32[]{:S(2)}) copy-start(bf16[8,1024]{1,0:T(8,128)(2,1)S(1)} %convert_element_type.58) | copy-start | bytes 49156
  954.8 82.3 %copy-start.4 = (f32[1,128,462]{1,2,0:T(8,128)S(1)}, f32[1,128,462]{1,2,0:T(8,128)}, u32[]{:S(2)}) copy-start(f32[1,128,462]{1,2,0:T(8,128)} %get-tuple-element.6) | copy-start | bytes 709636
  1035.5 1.6 copy-start.5
Sparse Core Ops, SparseCore 0:
  11.0 135.0 all-gather.1
  150.9 86.1 all-reduce.5
  242.1 685.4 reduce-scatter.1
  956.1 79.3 all-reduce.3
where the time goes:
time: 1080 us
  waiting for transfers between devices  930 us (86%)
  blocking collectives  95.5 us (9%)
  matrix products  16.9 us (2%)
  starting transfers between devices  15.2 us (1%)
  between operations  13.9 us (1%)
    reduce_scatter x1, waiting for transfers between devices, shards(): lax.psum_scatter(jnp.dot(hidden, down_weight, preferred_element_type=jnp....  651 us
    all_gather x1, waiting for transfers between devices, shards(): teacher_all = lax.all_gather(teacher_tokens, 'col', axis=0, tiled=True)  95.6 us
    psum x1, waiting for transfers between devices, shards(): gate_sum, up_sum = lax.psum((gate_part, up_part), 'row')  86.3 us
    psum x1, waiting for transfers between devices, shards(): hidden_grad = lax.psum(hidden_local, 'row')  79.5 us
    all_to_all x1, blocking collectives, shards(): lax.all_to_all(outgoing, 'col', split_axis=0, concat_axis=0, tiled=True)  38.3 us
    all_to_all x1, blocking collectives, shards(): lax.all_to_all(from_experts(row_grad, col_count, capacity), 'col', split_...  31.2 us
    all_to_all x1, blocking collectives, shards(): lax.all_to_all(grad_out, 'col', split_axis=0, concat_axis=0, tiled=True)  26 us
  transfers between devices with their start and end apart: 5, of which 5 were waited for; matrix products, arithmetic and copies ran while one was open for 1% of the time, Pallas kernels for 0%

commit v1 on v0

v1 whole, which is shorter than its diff:
```python
import functools

import jax
import jax.numpy as jnp
from jax import lax
from jax.experimental import pallas as pl
from jax.experimental.pallas import tpu as pltpu
from jax.sharding import PartitionSpec as P

MESH = pl.DeviceIdType.MESH
F32 = jnp.float32
BF16 = jnp.bfloat16

ROWS = 8
YS, ZS = 4, 16
COLS = YS * ZS
TOK = 8
WIDTH = 1024
LANES = 128
SUB = WIDTH // LANES
UNITS = 462
PAD = 512
CAP = 2
TOPK = 6
SLOTS = COLS * CAP
CHUNK = ZS * TOK
MINE = CHUNK // ROWS
BLOCK = TOK * SUB
MSG = CAP * SUB
SLOT_ROWS = COLS * MSG
STUDENT = YS
Y_OFFSETS = (0, 1, 3, 2)
TILE = 256


def dot(a, b):
    return jnp.dot(a, b, preferred_element_type=F32)


def dot_first(a, b):
    return lax.dot_general(a, b, (((0,), (0,)), ((), ())), preferred_element_type=F32)


def dot_last(a, b):
    return lax.dot_general(a, b, (((1,), (1,)), ((), ())), preferred_element_type=F32)


def to_lane_rows(rows):
    return jnp.concatenate([rows[:, j * LANES : (j + 1) * LANES] for j in range(SUB)], axis=0)


def from_lane_rows(block):
    return jnp.concatenate([block[j * TOK : (j + 1) * TOK, :] for j in range(SUB)], axis=1)


def kernel(
    teacher_ref,
    student_ref,
    gate_hbm,
    up_hbm,
    down_hbm,
    ids_ref,
    slots_ref,
    routes_ref,
    teacher_out,
    student_out,
    input_grad,
    gate_in,
    up_in,
    down_in,
    weight_sem,
    wide,
    down,
    tokens,
    placing,
    weighting,
    sent_slots,
    got_slots,
    spread,
    rows_in,
    part,
    part_got,
    hidden,
    pre,
    own_sum,
    y_send,
    y_got,
    z_send,
    z_got,
    back_send,
    back_got,
    loss_send,
    loss_got,
    hid_part,
    hid_got,
    grads,
    last_send,
    last_got,
    zg_send_sem,
    zg_recv_sem,
    yf_send_sem,
    yf_recv_sem,
    a2a_send_sem,
    a2a_recv_sem,
    rs_send_sem,
    rs_recv_sem,
    ag_send_sem,
    ag_recv_sem,
    yr_send_sem,
    yr_recv_sem,
    zr_send_sem,
    zr_recv_sem,
    ready_sem,
):
    r = lax.axis_index("row")
    c = lax.axis_index("col")
    x, core = r // 2, lax.rem(r, 2)
    y, z = c // ZS, lax.rem(c, ZS)

    def row_peer(m):
        return lax.rem(x + 1 + m // 2, 4) * 2 + lax.rem(core + 1 + lax.rem(m, 2), 2)

    def far_first(i):
        distance = ZS // 2 - (i + 1) // 2
        return lax.rem(z + distance * (1 - 2 * lax.rem(i + 1, 2)) + ZS, ZS)

    def col_peer(m):
        return lax.rem(y + 1 + lax.rem(m, YS), YS) * ZS + far_first(m // YS)

    def send(src, dst, send_sem, recv_sem, row, col):
        return pltpu.make_async_remote_copy(
            src_ref=src,
            dst_ref=dst,
            send_sem=send_sem,
            recv_sem=recv_sem,
            device_id=(row, col),
            device_id_type=MESH,
        )

    def wait_for(view, sem):
        pltpu.make_async_copy(view, view, sem).wait()

    weights = [
        pltpu.make_async_copy(a, b, weight_sem.at[i])
        for i, (a, b) in enumerate(((gate_hbm, gate_in), (up_hbm, up_in), (down_hbm, down_in)))
    ]
    for copy in weights:
        copy.start()
    barrier = pltpu.get_barrier_semaphore()

    @pl.loop(0, COLS - 1)
    def _(m):
        pl.semaphore_signal(barrier, inc=1, device_id=(r, col_peer(m)), device_id_type=MESH)

    @pl.loop(0, ROWS - 1)
    def _(m):
        pl.semaphore_signal(barrier, inc=1, device_id=(row_peer(m), c), device_id_type=MESH)

    tokens[c] = to_lane_rows(teacher_ref[...].astype(F32)).astype(BF16)
    targets = ids_ref[...] * CAP + slots_ref[...]
    routes = routes_ref[...].astype(F32)
    targets = jnp.concatenate([targets] * SUB, axis=0)
    routes = jnp.concatenate([routes] * SUB, axis=0)
    at = lax.broadcasted_iota(jnp.int32, (BLOCK, SLOT_ROWS), 1)
    lane_group = lax.broadcasted_iota(jnp.int32, (BLOCK, SLOT_ROWS), 0) // TOK
    slot_of = jnp.where(at % SUB == lane_group, at // SUB, -1)
    place = jnp.zeros((BLOCK, SLOT_ROWS), F32)
    weigh = jnp.zeros((BLOCK, SLOT_ROWS), F32)
    for k in range(TOPK):
        match = slot_of == targets[:, k : k + 1]
        place = jnp.where(match, 1.0, place)
        weigh = jnp.where(match, routes[:, k : k + 1], weigh)
    placing[...] = place.astype(BF16)
    weighting[...] = weigh.astype(BF16)
    student_rows = to_lane_rows(student_ref[...].astype(F32)).astype(BF16)
    sent_slots[...] = dot_first(placing[...], student_rows).astype(BF16)

    pl.semaphore_wait(barrier, COLS - 1 + ROWS - 1)

    def gather_z(i):
        to = y * ZS + far_first(i)
        return send(tokens.at[c], tokens.at[c], zg_send_sem, zg_recv_sem.at[z], r, to)

    @pl.loop(0, ZS - 1)
    def _(i):
        gather_z(i).start()

    def forward_y(zi):
        block = tokens.at[y * ZS + zi]
        for o in (2, 1, 3):
            to = lax.rem(y + o, YS) * ZS + z
            send(block, block, yf_send_sem, yf_recv_sem.at[YS - o], r, to).start()

    forward_y(z)

    def all_to_all(n, src, dst):
        @pl.loop(0, COLS - 1)
        def _(m):
            to = col_peer(m)
            send(
                src.at[pl.ds(pl.multiple_of(to * MSG, MSG), MSG)],
                dst.at[pl.ds(pl.multiple_of(c * MSG, MSG), MSG)],
                a2a_send_sem.at[n],
                a2a_recv_sem.at[n],
                r,
                to,
            ).start()

        own = pl.ds(pl.multiple_of(c * MSG, MSG), MSG)
        dst[own, :] = src[own, :]

    def all_to_all_wait(n, src, dst):
        most = pl.ds(0, (COLS - 1) * MSG)
        wait_for(dst.at[most], a2a_recv_sem.at[n])

    def all_to_all_done(n, src):
        most = pl.ds(0, (COLS - 1) * MSG)
        wait_for(src.at[most], a2a_send_sem.at[n])

    all_to_all(0, sent_slots, got_slots)

    wide[:, PAD - LANES : PAD] = jnp.zeros((WIDTH, LANES), BF16)
    wide[:, 2 * PAD - LANES :] = jnp.zeros((WIDTH, LANES), BF16)
    down[PAD - 64 :, :] = jnp.zeros((64, WIDTH), BF16)
    for copy in weights:
        copy.wait()
    wide[:, :UNITS] = gate_in[...]
    wide[:, PAD : PAD + UNITS] = up_in[...]
    down[:UNITS, :] = down_in[...]

    @pl.loop(0, ZS - 1)
    def _(i):
        zi = far_first(ZS - 2 - i)
        block = tokens.at[y * ZS + zi]
        wait_for(block, zg_recv_sem.at[zi])
        forward_y(zi)

    def send_rows(n, src, dst, chunk):
        @pl.loop(0, ROWS - 1)
        def _(m):
            to = row_peer(m)
            send(
                src.at[pl.ds(pl.multiple_of(to * MINE, MINE), MINE)],
                dst.at[r],
                rs_send_sem.at[n],
                rs_recv_sem.at[n],
                to,
                c,
            ).start()

        dst[r] = src[pl.ds(pl.multiple_of(r * MINE, MINE), MINE), :]

    def sum_rows(n, dst):
        wait_for(dst.at[pl.ds(0, ROWS - 1)], rs_recv_sem.at[n])
        total = dst[0].astype(F32)
        for i in range(1, ROWS):
            total = total + dst[i].astype(F32)
        return total

    def gather_rows(n, buf, rows):
        mine = pl.ds(pl.multiple_of(r * MINE, MINE), MINE)
        buf[mine, :] = rows

        @pl.loop(0, ROWS - 1)
        def _(m):
            send(
                buf.at[mine], buf.at[mine], ag_send_sem.at[n], ag_recv_sem.at[n], row_peer(m), c
            ).start()

    def gather_rows_wait(n, buf):
        wait_for(buf.at[pl.ds(0, (ROWS - 1) * MINE)], ag_recv_sem.at[n])

    def project(n):
        @pl.loop(0, 2 * PAD // TILE)
        def _(i):
            cols = pl.ds(pl.multiple_of(i * TILE, TILE), TILE)
            part[n, :, cols] = dot(rows_in[...], wide[:, cols]).astype(BF16)

        send_rows(n, part.at[n], part_got.at[n], n)

    def load_teacher(n):
        group = lax.rem(y + Y_OFFSETS[n], YS)
        if n > 0:
            block = tokens.at[pl.ds(group * ZS, ZS)]
            wait_for(block, yf_recv_sem.at[Y_OFFSETS[n]])
        blocks = tokens[pl.ds(group * ZS, ZS)].astype(F32).reshape(ZS, SUB, TOK, LANES)
        for j in range(SUB):
            rows_in[:, j * LANES : (j + 1) * LANES] = (
                blocks[:, j].reshape(CHUNK, LANES).astype(BF16)
            )

    def load_slots(got):
        spread[...] = got[...].astype(F32)
        for j in range(SUB):
            rows_in[:, j * LANES : (j + 1) * LANES] = spread[
                pl.ds(j, SLOTS, stride=SUB), :
            ].astype(BF16)

    def activate(n):
        total = sum_rows(n, part_got.at[n])
        gate, up = total[:, :PAD], total[:, PAD:]
        if n == STUDENT:
            pre[...] = total
        gather_rows(n, hidden.at[n], (gate / (1.0 + jnp.exp(-gate)) * up).astype(BF16))

    def store_slots(value, cols, first):
        for j in range(TILE // LANES):
            spread[pl.ds(first + j, SLOTS, stride=SUB), :] = value[:, j * LANES : (j + 1) * LANES]

    def produce_teacher(n):
        gather_rows_wait(n, hidden.at[n])
        for i in range(WIDTH // TILE):
            value = dot(hidden[n], down[:, i * TILE : (i + 1) * TILE])
            halves = [
                value[:, j * LANES : (j + 1) * LANES].reshape(ZS, TOK, LANES)
                for j in range(TILE // LANES)
            ]
            value = jnp.concatenate(halves, axis=1)
            rows = slice(i * 2 * TOK, (i + 1) * 2 * TOK)
            if n == 0:
                own_sum[:, rows, :] = value
            else:
                y_send[n - 1, :, rows, :] = value.astype(BF16)
        if n > 0:
            o = Y_OFFSETS[n]
            to = lax.rem(y + o, YS) * ZS + z

            @pl.loop(0, ZS)
            def _(i):
                zi = far_first(i)
                send(
                    y_send.at[n - 1, zi],
                    y_got.at[zi, n - 1],
                    yr_send_sem,
                    yr_recv_sem.at[zi],
                    r,
                    to,
                ).start()

    def produce_student():
        gather_rows_wait(STUDENT, hidden.at[STUDENT])
        for i in range(WIDTH // TILE):
            value = dot(hidden[STUDENT], down[:, i * TILE : (i + 1) * TILE])
            store_slots(value, i, i * (TILE // LANES))
        back_send[...] = spread[...].astype(BF16)
        all_to_all(1, back_send, back_got)

    for n in range(YS):
        load_teacher(n)
        project(n)
    activate(0)
    activate(1)
    all_to_all_wait(0, sent_slots, got_slots)
    load_slots(got_slots)
    project(STUDENT)
    activate(2)
    activate(3)
    produce_teacher(0)
    produce_teacher(1)
    activate(STUDENT)
    produce_teacher(2)
    produce_teacher(3)
    produce_student()

    @pl.loop(0, ZS)
    def _(i):
        zi = far_first(i)
        wait_for(y_got.at[zi], yr_recv_sem.at[zi])
        got = y_got[zi].astype(F32)
        total = own_sum[zi] + got[0] + got[1] + got[2]
        z_send[zi] = total.astype(BF16)

        @pl.when(i < ZS - 1)
        def _():
            to = y * ZS + zi
            send(z_send.at[zi], z_got.at[z], zr_send_sem, zr_recv_sem, r, to).start()

        @pl.when(i == ZS - 1)
        def _():
            z_got[zi] = total.astype(BF16)

    wait_for(z_got.at[pl.ds(0, ZS - 1)], zr_recv_sem)
    teacher = z_got[0].astype(F32)
    for i in range(1, ZS):
        teacher = teacher + z_got[i].astype(F32)
    teacher = teacher.astype(BF16).astype(F32)
    teacher_out[...] = from_lane_rows(teacher).astype(BF16)

    all_to_all_wait(1, back_send, back_got)
    student = dot(weighting[...], back_got[...]).astype(BF16).astype(F32)
    loss = (student - teacher).astype(BF16)
    loss_send[...] = dot_first(weighting[...], loss).astype(BF16)
    all_to_all(2, loss_send, loss_got)
    student_out[...] = from_lane_rows(student).astype(BF16)

    all_to_all_wait(2, loss_send, loss_got)
    load_slots(loss_got)

    for i in range(PAD // TILE):
        units = slice(i * TILE, (i + 1) * TILE)
        hid_part[:, units] = dot_last(rows_in[...], down[units, :]).astype(BF16)
    send_rows(YS + 1, hid_part, hid_got, 0)
    pre_gate, pre_up = pre[:, :PAD], pre[:, PAD:]
    logistic = 1.0 / (1.0 + jnp.exp(-pre_gate))
    slope = logistic * (1.0 + pre_gate * (1.0 - logistic))
    hidden_grad = sum_rows(YS + 1, hid_got)
    gate_grad = hidden_grad * pre_up * slope
    up_grad = hidden_grad * (pre_gate * logistic)
    both = jnp.concatenate([gate_grad, up_grad], axis=1).astype(BF16)
    gather_rows(YS + 1, grads, both)
    gather_rows_wait(YS + 1, grads)
    for i in range(WIDTH // TILE):
        value = dot_last(grads[...], wide[i * TILE : (i + 1) * TILE, :])
        store_slots(value, i, i * (TILE // LANES))
    last_send[...] = spread[...].astype(BF16)
    all_to_all(3, last_send, last_got)
    all_to_all_wait(3, last_send, last_got)
    grad = dot(placing[...], last_got[...])
    input_grad[...] = from_lane_rows(grad).astype(BF16)

    wait_for(tokens.at[pl.ds(0, ZS - 1)], zg_send_sem)
    wait_for(tokens.at[pl.ds(0, 3 * ZS)], yf_send_sem)
    for n, src in enumerate((sent_slots, back_send, loss_send, last_send)):
        all_to_all_done(n, src)
    for n in range(YS + 1):
        wait_for(part.at[n, pl.ds(0, (ROWS - 1) * MINE)], rs_send_sem.at[n])
        wait_for(hidden.at[n, pl.ds(0, (ROWS - 1) * MINE)], ag_send_sem.at[n])
    wait_for(hid_part.at[pl.ds(0, (ROWS - 1) * MINE)], rs_send_sem.at[YS + 1])
    wait_for(grads.at[pl.ds(0, (ROWS - 1) * MINE)], ag_send_sem.at[YS + 1])
    wait_for(y_send, yr_send_sem)
    wait_for(z_send.at[pl.ds(0, ZS - 1)], zr_send_sem)


def shards(*operands):
    vmem = pl.BlockSpec(memory_space=pltpu.VMEM)
    hbm = pl.BlockSpec(memory_space=pl.ANY)
    out = jax.ShapeDtypeStruct((TOK, WIDTH), BF16)
    sems = pltpu.SemaphoreType.DMA
    return pl.pallas_call(
        kernel,
        out_shape=(out, out, out),
        in_specs=[vmem, vmem, hbm, hbm, hbm, vmem, vmem, vmem],
        out_specs=(vmem, vmem, vmem),
        scratch_shapes=[
            pltpu.VMEM((WIDTH, UNITS), BF16),
            pltpu.VMEM((WIDTH, UNITS), BF16),
            pltpu.VMEM((UNITS, WIDTH), BF16),
            sems((3,)),
            pltpu.VMEM((WIDTH, 2 * PAD), BF16),
            pltpu.VMEM((PAD, WIDTH), BF16),
            pltpu.VMEM((COLS, BLOCK, LANES), BF16),
            pltpu.VMEM((BLOCK, SLOT_ROWS), BF16),
            pltpu.VMEM((BLOCK, SLOT_ROWS), BF16),
            pltpu.VMEM((SLOT_ROWS, LANES), BF16),
            pltpu.VMEM((SLOT_ROWS, LANES), BF16),
            pltpu.VMEM((SLOT_ROWS, LANES), F32),
            pltpu.VMEM((CHUNK, WIDTH), BF16),
            pltpu.VMEM((YS + 1, CHUNK, 2 * PAD), BF16),
            pltpu.VMEM((YS + 1, ROWS, MINE, 2 * PAD), BF16),
            pltpu.VMEM((YS + 1, CHUNK, PAD), BF16),
            pltpu.VMEM((MINE, 2 * PAD), F32),
            pltpu.VMEM((ZS, BLOCK, LANES), F32),
            pltpu.VMEM((YS - 1, ZS, BLOCK, LANES), BF16),
            pltpu.VMEM((ZS, YS - 1, BLOCK, LANES), BF16),
            pltpu.VMEM((ZS, BLOCK, LANES), BF16),
            pltpu.VMEM((ZS, BLOCK, LANES), BF16),
            pltpu.VMEM((SLOT_ROWS, LANES), BF16),
            pltpu.VMEM((SLOT_ROWS, LANES), BF16),
            pltpu.VMEM((SLOT_ROWS, LANES), BF16),
            pltpu.VMEM((SLOT_ROWS, LANES), BF16),
            pltpu.VMEM((CHUNK, PAD), BF16),
            pltpu.VMEM((ROWS, MINE, PAD), BF16),
            pltpu.VMEM((CHUNK, 2 * PAD), BF16),
            pltpu.VMEM((SLOT_ROWS, LANES), BF16),
            pltpu.VMEM((SLOT_ROWS, LANES), BF16),
            sems,
            sems((ZS,)),
            sems,
            sems((YS,)),
            sems((4,)),
            sems((4,)),
            sems((YS + 2,)),
            sems((YS + 2,)),
            sems((YS + 2,)),
            sems((YS + 2,)),
            sems,
            sems((ZS,)),
            sems,
            sems,
            pltpu.SemaphoreType.REGULAR,
        ],
        compiler_params=pltpu.CompilerParams(
            collective_id=0, has_side_effects=True, vmem_limit_bytes=48 * 2**20
        ),
    )(*operands)


def solution(mesh):
    return jax.shard_map(
        shards,
        mesh=mesh,
        in_specs=(
            P("col", "row"),
            P("col", "row"),
            P("row", "col"),
            P("row", "col"),
            P("col", "row"),
            P("col", None),
            P("col", None),
            P("col", None),
        ),
        out_specs=(P("col", "row"), P("col", "row"), P("col", "row")),
        check_vma=False,
    )
```

time: 1080 us -> 137 us (0.13)
  waiting for transfers between devices: 930 us -> 0 us
  Pallas kernels: 0 us -> 131 us
  blocking collectives: 95.5 us -> 0 us
  matrix products: 16.9 us -> 0 us
  starting transfers between devices: 15.2 us -> 0 us
  between operations: 13.9 us -> 0.75 us
    reduce_scatter x1 -> x0, waiting for transfers between devices: 651 us -> none  [shards(): lax.psum_scatter(jnp.dot(hidden, down_weight, preferred_element_type=jnp....]
    psum x2 -> x0, waiting for transfers between devices: 166 us -> none  [the longest x1 86.3 us: shards(): gate_sum, up_sum = lax.psum((gate_part, up_part), 'row')]
    pallas_call x0 -> x1, Pallas kernels: none -> 131 us  [shards(): pl.pallas_call(kernel, out_shape=(out, out, out), in_specs=[vmem, vmem, h...]
    all_gather x1 -> x0, waiting for transfers between devices: 95.6 us -> none  [shards(): teacher_all = lax.all_gather(teacher_tokens, 'col', axis=0, tiled=True)]
    all_to_all x3 -> x0, blocking collectives: 95.5 us -> none  [the longest x1 38.3 us: shards(): lax.all_to_all(outgoing, 'col', split_axis=0, concat_axis=0, tiled=True)]
    all_to_all x1 -> x0, waiting for transfers between devices: 17.2 us -> none  [shards(): lax.all_to_all(from_experts(produced, col_count, capacity), 'col', split_...]
    dot_general x13 -> x0, matrix products: 16.9 us -> none  [the longest x1 3.55 us: shards(): jnp.dot(hidden, down_weight, preferred_element_type=jnp.float32)]
    all_to_all x1 -> x0, starting transfers between devices: 15 us -> none  [shards(): lax.all_to_all(from_experts(produced, col_count, capacity), 'col', split_...]
  transfers between devices with their start and end apart: 5 -> 0, of which waited for: 5 -> 0; matrix products, arithmetic and copies ran while one was open for 1% -> 0% of each run, Pallas kernels for 0% -> 0%
where the time goes in v1:
time: 137 us
  Pallas kernels  131 us (96%)
  local copies, waits for them, and re-layouts  4.87 us (4%)
    pallas_call x1, Pallas kernels, shards(): pl.pallas_call(kernel, out_shape=(out, out, out), in_specs=[vmem, vmem, h...  131 us
    unnamed x17, local copies, waits for them, and re-layouts  4.87 us

profile of v1, /device:TPU:1, one launch (start us, length us, event | category | flops | bytes accessed | tf_op | source)
XLA Modules:
  0.0 136.6 jit_solution(8400211090477985392)
XLA Ops:
  0.6 1.5 %copy.11.gate_hbm = bf16[1024,462]{1,0:T(8,128)(2,1)S(1)} copy(bf16[1024,462]{0,1:T(8,128)(2,1)} %param.10) | data formatting | bytes 1892352 | tf_op args[2]
  2.1 0.0 copy-start
  2.1 0.0 copy-start.1
  2.1 0.0 copy-start.2
  2.1 0.0 copy-start.3
  2.2 0.0 copy-start.4
  2.2 0.0 copy-start.5
  2.2 1.5 %copy.12.up_hbm = bf16[1024,462]{1,0:T(8,128)(2,1)S(1)} copy(bf16[1024,462]{0,1:T(8,128)(2,1)} %param.11) | data formatting | bytes 1892352 | tf_op args[3]
  3.7 0.0 copy-done
  3.7 0.0 copy-done.1
  3.8 0.0 copy-done.2
  3.8 0.0 copy-done.3
  3.8 0.0 copy-done.4
  3.8 0.0 copy-done.5
  3.8 131.0 %shard_map.103 = (bf16[8,1024]{1,0:T(8,128)(2,1)S(1)}, bf16[8,1024]{1,0:T(8,128)(2,1)S(1)}, bf16[8,1024]{1,0:T(8,128)(2,1)S(1)}) custom-call(bf16[8,1024]{1,0:T(8,128)(2,1)S(1)} %copy-done.1, bf16[8,1024]{1,0:T(8,128)(2,1)S(1)} %copy-done.2, bf16[1024,462]{1,0:T(8,128)(2,1)S(1)} %copy.11.gate_hbm, bf16[1024,462]{1,0:T(8,128)(2,1)S(1)} %copy.12.up_hbm, ...), custom_call_target="tpu_custom_call" | custom-call | tf_op jit(solution)/shard_map/pallas_call | solution.py:439
  134.8 0.6 copy.16
  135.4 0.6 copy.17
  136.0 0.6 copy.18
Async XLA Ops:
  2.1 1.6 %copy-start = (bf16[462,1024]{1,0:T(8,128)(2,1)S(1)}, bf16[462,1024]{1,0:T(8,128)(2,1)}, u32[]{:S(2)}) copy-start(bf16[462,1024]{1,0:T(8,128)(2,1)} %down_hbm.1) | copy-start | bytes 2838532
  2.1 1.6 %copy-start.1 = (bf16[8,1024]{1,0:T(8,128)(2,1)S(1)}, bf16[8,1024]{1,0:T(8,128)(2,1)}, u32[]{:S(2)}) copy-start(bf16[8,1024]{1,0:T(8,128)(2,1)} %teacher_ref.1) | copy-start | bytes 49156
  2.1 1.6 %copy-start.2 = (bf16[8,1024]{1,0:T(8,128)(2,1)S(1)}, bf16[8,1024]{1,0:T(8,128)(2,1)}, u32[]{:S(2)}) copy-start(bf16[8,1024]{1,0:T(8,128)(2,1)} %student_ref.1) | copy-start | bytes 49156
  2.1 1.6 %copy-start.3 = (s32[8,6]{1,0:T(8,128)S(1)}, s32[8,6]{1,0:T(8,128)}, u32[]{:S(2)}) copy-start(s32[8,6]{1,0:T(8,128)} %ids_ref.1) | copy-start | bytes 580
  2.2 1.6 %copy-start.4 = (s32[8,6]{1,0:T(8,128)S(1)}, s32[8,6]{1,0:T(8,128)}, u32[]{:S(2)}) copy-start(s32[8,6]{1,0:T(8,128)} %slots_ref.1) | copy-start | bytes 580
  2.2 1.6 %copy-start.5 = (bf16[8,6]{1,0:T(8,128)(2,1)S(1)}, bf16[8,6]{1,0:T(8,128)(2,1)}, u32[]{:S(2)}) copy-start(bf16[8,6]{1,0:T(8,128)(2,1)} %routes_ref.1) | copy-start | bytes 292

commit v2 on v1

--- a/solution.py
+++ b/solution.py
@@ -37,14 +37,6 @@
     return jnp.dot(a, b, preferred_element_type=F32)
 
 
-def dot_first(a, b):
-    return lax.dot_general(a, b, (((0,), (0,)), ((), ())), preferred_element_type=F32)
-
-
-def dot_last(a, b):
-    return lax.dot_general(a, b, (((1,), (1,)), ((), ())), preferred_element_type=F32)
-
-
 def to_lane_rows(rows):
     return jnp.concatenate([rows[:, j * LANES : (j + 1) * LANES] for j in range(SUB)], axis=0)
 
@@ -54,26 +46,35 @@
 
 
 def kernel(
-    teacher_ref,
-    student_ref,
+    teacher_hbm,
+    student_hbm,
     gate_hbm,
     up_hbm,
     down_hbm,
+    ids_hbm,
+    slots_hbm,
+    routes_hbm,
+    teacher_out,
+    student_out,
+    input_grad,
+    teacher_ref,
+    student_ref,
+    gate_in,
+    up_in,
+    down_in,
     ids_ref,
     slots_ref,
     routes_ref,
-    teacher_out,
-    student_out,
-    input_grad,
-    gate_in,
-    up_in,
-    down_in,
-    weight_sem,
+    input_sem,
     wide,
+    wide_t,
     down,
+    down_t,
     tokens,
     placing,
+    placing_t,
     weighting,
+    weighting_t,
     sent_slots,
     got_slots,
     spread,
@@ -140,50 +141,117 @@
     def wait_for(view, sem):
         pltpu.make_async_copy(view, view, sem).wait()
 
-    weights = [
-        pltpu.make_async_copy(a, b, weight_sem.at[i])
-        for i, (a, b) in enumerate(((gate_hbm, gate_in), (up_hbm, up_in), (down_hbm, down_in)))
+    owed, left = {}, []
+
+    def owe(name, arrive, leave):
+        owed[name] = lambda: wait_for(*arrive)
+        left.append(lambda: wait_for(*leave))
+
+    def take(*name):
+        owed.pop(name)()
+
+    inputs = [
+        pltpu.make_async_copy(a, b, input_sem.at[i])
+        for i, (a, b) in enumerate(
+            (
+                (teacher_hbm, teacher_ref),
+                (student_hbm, student_ref),
+                (ids_hbm, ids_ref),
+                (slots_hbm, slots_ref),
+                (routes_hbm, routes_ref),
+                (gate_hbm, gate_in),
+                (up_hbm, up_in),
+                (down_hbm, down_in),
+            )
+        )
     ]
-    for copy in weights:
+    for copy in inputs:
         copy.start()
     barrier = pltpu.get_barrier_semaphore()
 
-    @pl.loop(0, COLS - 1)
-    def _(m):
-        pl.semaphore_signal(barrier, inc=1, device_id=(r, col_peer(m)), device_id_type=MESH)
+    @pl.loop(0, ZS - 1)
+    def _(i):
+        to = y * ZS + far_first(i)
+        pl.semaphore_signal(barrier, inc=1, device_id=(r, to), device_id_type=MESH)
+
+    for o in range(1, YS):
+        to = lax.rem(y + o, YS) * ZS + z
+        pl.semaphore_signal(barrier, inc=1, device_id=(r, to), device_id_type=MESH)
 
     @pl.loop(0, ROWS - 1)
     def _(m):
         pl.semaphore_signal(barrier, inc=1, device_id=(row_peer(m), c), device_id_type=MESH)
 
+    for copy in inputs[:5]:
+        copy.wait()
     tokens[c] = to_lane_rows(teacher_ref[...].astype(F32)).astype(BF16)
-    targets = ids_ref[...] * CAP + slots_ref[...]
-    routes = routes_ref[...].astype(F32)
-    targets = jnp.concatenate([targets] * SUB, axis=0)
-    routes = jnp.concatenate([routes] * SUB, axis=0)
-    at = lax.broadcasted_iota(jnp.int32, (BLOCK, SLOT_ROWS), 1)
-    lane_group = lax.broadcasted_iota(jnp.int32, (BLOCK, SLOT_ROWS), 0) // TOK
-    slot_of = jnp.where(at % SUB == lane_group, at // SUB, -1)
-    place = jnp.zeros((BLOCK, SLOT_ROWS), F32)
-    weigh = jnp.zeros((BLOCK, SLOT_ROWS), F32)
-    for k in range(TOPK):
-        match = slot_of == targets[:, k : k + 1]
-        place = jnp.where(match, 1.0, place)
-        weigh = jnp.where(match, routes[:, k : k + 1], weigh)
-    placing[...] = place.astype(BF16)
-    weighting[...] = weigh.astype(BF16)
+
+    for ref, first in ((wide_t, 0), (wide_t, PAD), (down, 0)):
+        ref[first + PAD - 64 : first + PAD, :] = jnp.zeros((64, WIDTH), BF16)
+    for copy in inputs[5:]:
+        copy.wait()
+    wide_t[:UNITS, :] = gate_in[...]
+    wide_t[PAD : PAD + UNITS, :] = up_in[...]
+    down[:UNITS, :] = down_in[...]
+
+    @pl.loop(0, 2 * PAD // TILE)
+    def _(i):
+        units = pl.ds(pl.multiple_of(i * TILE, TILE), TILE)
+        for k in range(WIDTH // TILE):
+            wide[k * TILE : (k + 1) * TILE, units] = wide_t[units, k * TILE : (k + 1) * TILE].T
+
+    targets = (ids_ref[...] * CAP + slots_ref[...]).astype(F32)
+    choices = jnp.concatenate([targets, routes_ref[...].astype(F32)], axis=1)
+    choices = jnp.concatenate([choices, jnp.zeros((TOK, LANES - 2 * TOPK), F32)], axis=1)
+    choices = jnp.concatenate([choices] * SUB, axis=0)
+    flipped = choices.T
+
+    def match(slot_of, targets, routes, place_ref, weigh_ref, at):
+        place = jnp.zeros(slot_of.shape, F32)
+        weigh = jnp.zeros(slot_of.shape, F32)
+        for k in range(TOPK):
+            hit = slot_of == targets(k)
+            place = jnp.where(hit, 1.0, place)
+            weigh = jnp.where(hit, routes(k), weigh)
+        place_ref[at] = place.astype(BF16)
+        weigh_ref[at] = weigh.astype(BF16)
+
+    for i in range(SLOT_ROWS // LANES):
+        shape = (BLOCK, LANES)
+        row = lax.broadcasted_iota(jnp.int32, shape, 0)
+        col = lax.broadcasted_iota(jnp.int32, shape, 1) + i * LANES
+        slot_of = jnp.where((col & (SUB - 1)) == (row >> 3), col >> 3, -1).astype(F32)
+        match(
+            slot_of,
+            lambda k: choices[:, k : k + 1],
+            lambda k: choices[:, TOPK + k : TOPK + k + 1],
+            placing,
+            weighting,
+            (slice(None), slice(i * LANES, (i + 1) * LANES)),
+        )
+        shape = (LANES, BLOCK)
+        row = lax.broadcasted_iota(jnp.int32, shape, 0) + i * LANES
+        col = lax.broadcasted_iota(jnp.int32, shape, 1)
+        slot_of = jnp.where((row & (SUB - 1)) == (col >> 3), row >> 3, -1).astype(F32)
+        match(
+            slot_of,
+            lambda k: flipped[k : k + 1, :],
+            lambda k: flipped[TOPK + k : TOPK + k + 1, :],
+            placing_t,
+            weighting_t,
+            (slice(i * LANES, (i + 1) * LANES), slice(None)),
+        )
     student_rows = to_lane_rows(student_ref[...].astype(F32)).astype(BF16)
-    sent_slots[...] = dot_first(placing[...], student_rows).astype(BF16)
-
-    pl.semaphore_wait(barrier, COLS - 1 + ROWS - 1)
+    sent_slots[...] = dot(placing_t[...], student_rows).astype(BF16)
+
+    pl.semaphore_wait(barrier, ZS + YS - 2 + ROWS - 1)
 
     def gather_z(i):
-        to = y * ZS + far_first(i)
+        to = y * ZS + lax.rem(z + i, ZS)
         return send(tokens.at[c], tokens.at[c], zg_send_sem, zg_recv_sem.at[z], r, to)
 
-    @pl.loop(0, ZS - 1)
-    def _(i):
-        gather_z(i).start()
+    for o in [1, 15, 2, 14, 3, 13, 4, 12, 5, 11, 6, 10, 7, 9, 8]:
+        gather_z(o).start()
 
     def forward_y(zi):
         block = tokens.at[y * ZS + zi]
@@ -191,7 +259,14 @@
             to = lax.rem(y + o, YS) * ZS + z
             send(block, block, yf_send_sem, yf_recv_sem.at[YS - o], r, to).start()
 
+    left.append(lambda: wait_for(tokens.at[pl.ds(0, ZS - 1)], zg_send_sem))
+    left.append(lambda: wait_for(tokens.at[pl.ds(0, 3 * ZS)], yf_send_sem))
     forward_y(z)
+
+    for o in range(1, YS):
+        to = lax.rem(y + o, YS) * ZS + z
+        pl.semaphore_signal(ready_sem, inc=1, device_id=(r, to), device_id_type=MESH)
+    pl.semaphore_wait(ready_sem, YS - 1)
 
     def all_to_all(n, src, dst):
         @pl.loop(0, COLS - 1)
@@ -208,34 +283,24 @@
 
         own = pl.ds(pl.multiple_of(c * MSG, MSG), MSG)
         dst[own, :] = src[own, :]
-
-    def all_to_all_wait(n, src, dst):
         most = pl.ds(0, (COLS - 1) * MSG)
-        wait_for(dst.at[most], a2a_recv_sem.at[n])
-
-    def all_to_all_done(n, src):
-        most = pl.ds(0, (COLS - 1) * MSG)
-        wait_for(src.at[most], a2a_send_sem.at[n])
-
-    all_to_all(0, sent_slots, got_slots)
-
-    wide[:, PAD - LANES : PAD] = jnp.zeros((WIDTH, LANES), BF16)
-    wide[:, 2 * PAD - LANES :] = jnp.zeros((WIDTH, LANES), BF16)
-    down[PAD - 64 :, :] = jnp.zeros((64, WIDTH), BF16)
-    for copy in weights:
-        copy.wait()
-    wide[:, :UNITS] = gate_in[...]
-    wide[:, PAD : PAD + UNITS] = up_in[...]
-    down[:UNITS, :] = down_in[...]
-
-    @pl.loop(0, ZS - 1)
-    def _(i):
-        zi = far_first(ZS - 2 - i)
+        owe(("slots", n), (dst.at[most], a2a_recv_sem.at[n]), (src.at[most], a2a_send_sem.at[n]))
+
+    for o in [1, 15, 2, 14, 3, 13, 4, 12, 5, 11, 6, 10, 7, 9, 8]:
+        zi = lax.rem(z + o, ZS)
         block = tokens.at[y * ZS + zi]
         wait_for(block, zg_recv_sem.at[zi])
         forward_y(zi)
 
-    def send_rows(n, src, dst, chunk):
+    all_to_all(0, sent_slots, got_slots)
+
+    for n in range(1, YS):
+        group = lax.rem(y + Y_OFFSETS[n], YS)
+        block = tokens.at[pl.ds(group * ZS, ZS)]
+        owed["tokens", n] = functools.partial(wait_for, block, yf_recv_sem.at[Y_OFFSETS[n]])
+
+
+    def send_rows(n, src, dst):
         @pl.loop(0, ROWS - 1)
         def _(m):
             to = row_peer(m)
@@ -249,9 +314,15 @@
             ).start()
 
         dst[r] = src[pl.ds(pl.multiple_of(r * MINE, MINE), MINE), :]
+        leave = src.at[pl.ds(0, (ROWS - 1) * MINE)]
+        owe(
+            ("sum", n),
+            (dst.at[pl.ds(0, ROWS - 1)], rs_recv_sem.at[n]),
+            (leave, rs_send_sem.at[n]),
+        )
 
     def sum_rows(n, dst):
-        wait_for(dst.at[pl.ds(0, ROWS - 1)], rs_recv_sem.at[n])
+        take("sum", n)
         total = dst[0].astype(F32)
         for i in range(1, ROWS):
             total = total + dst[i].astype(F32)
@@ -267,8 +338,8 @@
                 buf.at[mine], buf.at[mine], ag_send_sem.at[n], ag_recv_sem.at[n], row_peer(m), c
             ).start()
 
-    def gather_rows_wait(n, buf):
-        wait_for(buf.at[pl.ds(0, (ROWS - 1) * MINE)], ag_recv_sem.at[n])
+        most = buf.at[pl.ds(0, (ROWS - 1) * MINE)]
+        owe(("gather", n), (most, ag_recv_sem.at[n]), (most, ag_send_sem.at[n]))
 
     def project(n):
         @pl.loop(0, 2 * PAD // TILE)
@@ -276,13 +347,12 @@
             cols = pl.ds(pl.multiple_of(i * TILE, TILE), TILE)
             part[n, :, cols] = dot(rows_in[...], wide[:, cols]).astype(BF16)
 
-        send_rows(n, part.at[n], part_got.at[n], n)
+        send_rows(n, part.at[n], part_got.at[n])
 
     def load_teacher(n):
         group = lax.rem(y + Y_OFFSETS[n], YS)
         if n > 0:
-            block = tokens.at[pl.ds(group * ZS, ZS)]
-            wait_for(block, yf_recv_sem.at[Y_OFFSETS[n]])
+            take("tokens", n)
         blocks = tokens[pl.ds(group * ZS, ZS)].astype(F32).reshape(ZS, SUB, TOK, LANES)
         for j in range(SUB):
             rows_in[:, j * LANES : (j + 1) * LANES] = (
@@ -308,7 +378,7 @@
             spread[pl.ds(first + j, SLOTS, stride=SUB), :] = value[:, j * LANES : (j + 1) * LANES]
 
     def produce_teacher(n):
-        gather_rows_wait(n, hidden.at[n])
+        take("gather", n)
         for i in range(WIDTH // TILE):
             value = dot(hidden[n], down[:, i * TILE : (i + 1) * TILE])
             halves = [
@@ -324,6 +394,7 @@
         if n > 0:
             o = Y_OFFSETS[n]
             to = lax.rem(y + o, YS) * ZS + z
+            left.append(lambda: wait_for(y_send.at[n - 1], yr_send_sem))
 
             @pl.loop(0, ZS)
             def _(i):
@@ -338,7 +409,7 @@
                 ).start()
 
     def produce_student():
-        gather_rows_wait(STUDENT, hidden.at[STUDENT])
+        take("gather", STUDENT)
         for i in range(WIDTH // TILE):
             value = dot(hidden[STUDENT], down[:, i * TILE : (i + 1) * TILE])
             store_slots(value, i, i * (TILE // LANES))
@@ -350,17 +421,17 @@
         project(n)
     activate(0)
     activate(1)
-    all_to_all_wait(0, sent_slots, got_slots)
+    take("slots", 0)
     load_slots(got_slots)
     project(STUDENT)
     activate(2)
     activate(3)
-    produce_teacher(0)
     produce_teacher(1)
+    produce_teacher(2)
     activate(STUDENT)
-    produce_teacher(2)
     produce_teacher(3)
     produce_student()
+    produce_teacher(0)
 
     @pl.loop(0, ZS)
     def _(i):
@@ -379,6 +450,14 @@
         def _():
             z_got[zi] = total.astype(BF16)
 
+    left.append(lambda: wait_for(z_send.at[pl.ds(0, ZS - 1)], zr_send_sem))
+
+    @pl.loop(0, PAD // TILE)
+    def _(i):
+        units = pl.ds(pl.multiple_of(i * TILE, TILE), TILE)
+        for k in range(WIDTH // TILE):
+            down_t[k * TILE : (k + 1) * TILE, units] = down[units, k * TILE : (k + 1) * TILE].T
+
     wait_for(z_got.at[pl.ds(0, ZS - 1)], zr_recv_sem)
     teacher = z_got[0].astype(F32)
     for i in range(1, ZS):
@@ -386,20 +465,20 @@
     teacher = teacher.astype(BF16).astype(F32)
     teacher_out[...] = from_lane_rows(teacher).astype(BF16)
 
-    all_to_all_wait(1, back_send, back_got)
+    take("slots", 1)
     student = dot(weighting[...], back_got[...]).astype(BF16).astype(F32)
     loss = (student - teacher).astype(BF16)
-    loss_send[...] = dot_first(weighting[...], loss).astype(BF16)
+    loss_send[...] = dot(weighting_t[...], loss).astype(BF16)
     all_to_all(2, loss_send, loss_got)
     student_out[...] = from_lane_rows(student).astype(BF16)
 
-    all_to_all_wait(2, loss_send, loss_got)
+    take("slots", 2)
     load_slots(loss_got)
 
     for i in range(PAD // TILE):
         units = slice(i * TILE, (i + 1) * TILE)
-        hid_part[:, units] = dot_last(rows_in[...], down[units, :]).astype(BF16)
-    send_rows(YS + 1, hid_part, hid_got, 0)
+        hid_part[:, units] = dot(rows_in[...], down_t[:, units]).astype(BF16)
+    send_rows(YS + 1, hid_part, hid_got)
     pre_gate, pre_up = pre[:, :PAD], pre[:, PAD:]
     logistic = 1.0 / (1.0 + jnp.exp(-pre_gate))
     slope = logistic * (1.0 + pre_gate * (1.0 - logistic))
@@ -408,49 +487,49 @@
     up_grad = hidden_grad * (pre_gate * logistic)
     both = jnp.concatenate([gate_grad, up_grad], axis=1).astype(BF16)
     gather_rows(YS + 1, grads, both)
-    gather_rows_wait(YS + 1, grads)
+    take("gather", YS + 1)
     for i in range(WIDTH // TILE):
-        value = dot_last(grads[...], wide[i * TILE : (i + 1) * TILE, :])
+        value = dot(grads[...], wide_t[:, i * TILE : (i + 1) * TILE])
         store_slots(value, i, i * (TILE // LANES))
     last_send[...] = spread[...].astype(BF16)
     all_to_all(3, last_send, last_got)
-    all_to_all_wait(3, last_send, last_got)
+    take("slots", 3)
     grad = dot(placing[...], last_got[...])
     input_grad[...] = from_lane_rows(grad).astype(BF16)
 
-    wait_for(tokens.at[pl.ds(0, ZS - 1)], zg_send_sem)
-    wait_for(tokens.at[pl.ds(0, 3 * ZS)], yf_send_sem)
-    for n, src in enumerate((sent_slots, back_send, loss_send, last_send)):
-        all_to_all_done(n, src)
-    for n in range(YS + 1):
-        wait_for(part.at[n, pl.ds(0, (ROWS - 1) * MINE)], rs_send_sem.at[n])
-        wait_for(hidden.at[n, pl.ds(0, (ROWS - 1) * MINE)], ag_send_sem.at[n])
-    wait_for(hid_part.at[pl.ds(0, (ROWS - 1) * MINE)], rs_send_sem.at[YS + 1])
-    wait_for(grads.at[pl.ds(0, (ROWS - 1) * MINE)], ag_send_sem.at[YS + 1])
-    wait_for(y_send, yr_send_sem)
-    wait_for(z_send.at[pl.ds(0, ZS - 1)], zr_send_sem)
-
-
-def shards(*operands):
+    for wait in left:
+        wait()
+
+
+def shards(teacher, student, gate, up, down, ids, slots, routes):
     vmem = pl.BlockSpec(memory_space=pltpu.VMEM)
-    hbm = pl.BlockSpec(memory_space=pl.ANY)
+    hbm = pl.BlockSpec(memory_space=pltpu.HBM)
     out = jax.ShapeDtypeStruct((TOK, WIDTH), BF16)
     sems = pltpu.SemaphoreType.DMA
     return pl.pallas_call(
         kernel,
         out_shape=(out, out, out),
-        in_specs=[vmem, vmem, hbm, hbm, hbm, vmem, vmem, vmem],
+        in_specs=[hbm] * 8,
         out_specs=(vmem, vmem, vmem),
         scratch_shapes=[
-            pltpu.VMEM((WIDTH, UNITS), BF16),
-            pltpu.VMEM((WIDTH, UNITS), BF16),
+            pltpu.VMEM((TOK, WIDTH), BF16),
+            pltpu.VMEM((TOK, WIDTH), BF16),
             pltpu.VMEM((UNITS, WIDTH), BF16),
-            sems((3,)),
+            pltpu.VMEM((UNITS, WIDTH), BF16),
+            pltpu.VMEM((UNITS, WIDTH), BF16),
+            pltpu.VMEM((TOK, TOPK), jnp.int32),
+            pltpu.VMEM((TOK, TOPK), jnp.int32),
+            pltpu.VMEM((TOK, TOPK), BF16),
+            sems((8,)),
             pltpu.VMEM((WIDTH, 2 * PAD), BF16),
+            pltpu.VMEM((2 * PAD, WIDTH), BF16),
             pltpu.VMEM((PAD, WIDTH), BF16),
+            pltpu.VMEM((WIDTH, PAD), BF16),
             pltpu.VMEM((COLS, BLOCK, LANES), BF16),
             pltpu.VMEM((BLOCK, SLOT_ROWS), BF16),
+            pltpu.VMEM((SLOT_ROWS, BLOCK), BF16),
             pltpu.VMEM((BLOCK, SLOT_ROWS), BF16),
+            pltpu.VMEM((SLOT_ROWS, BLOCK), BF16),
             pltpu.VMEM((SLOT_ROWS, LANES), BF16),
             pltpu.VMEM((SLOT_ROWS, LANES), BF16),
             pltpu.VMEM((SLOT_ROWS, LANES), F32),
@@ -490,9 +569,9 @@
             pltpu.SemaphoreType.REGULAR,
         ],
         compiler_params=pltpu.CompilerParams(
-            collective_id=0, has_side_effects=True, vmem_limit_bytes=48 * 2**20
+            collective_id=0, has_side_effects=True, vmem_limit_bytes=64 * 2**20
         ),
-    )(*operands)
+    )(teacher, student, gate.T, up.T, down, ids, slots, routes)
 
 
 def solution(mesh):

time: 137 us -> 127 us (0.927)
  Pallas kernels: 131 us -> 123 us
  local copies, waits for them, and re-layouts: 4.87 us -> 2.66 us
    pallas_call x1, Pallas kernels: 131 us -> 123 us  [shards(): pl.pallas_call(kernel, out_shape=(out, out, out), in_specs=[hbm] * 8, out...]
    unnamed x17 -> x7, local copies, waits for them, and re-layouts: 4.87 us -> 2.66 us
where the time goes in v2:
time: 127 us
  Pallas kernels  123 us (97%)
  local copies, waits for them, and re-layouts  2.66 us (2%)
    pallas_call x1, Pallas kernels, shards(): pl.pallas_call(kernel, out_shape=(out, out, out), in_specs=[hbm] * 8, out...  123 us
    unnamed x7, local copies, waits for them, and re-layouts  2.66 us

profile of v2, /device:TPU:1, one launch (start us, length us, event | category | flops | bytes accessed | tf_op | source)
XLA Modules:
  0.0 126.8 jit_solution(9268914056975182466)
XLA Ops:
  0.6 123.5 %shard_map.103 = (bf16[8,1024]{1,0:T(8,128)(2,1)}, bf16[8,1024]{1,0:T(8,128)(2,1)}, bf16[8,1024]{1,0:T(8,128)(2,1)}) custom-call(bf16[8,1024]{1,0:T(8,128)(2,1)} %teacher_hbm.1, bf16[8,1024]{1,0:T(8,128)(2,1)} %student_hbm.1, bf16[462,1024]{1,0:T(8,128)(2,1)} %bitcast.2, bf16[462,1024]{1,0:T(8,128)(2,1)} %bitcast.3, bf16[462,1024]{1,0:T(8,128)(2,1)} %down_hbm.1, ...), custom_call_target="tpu_custom_call" | custom-call | tf_op jit(solution)/shard_map/pallas_call | solution.py:509
  124.1 0.0 copy-start.1
  124.1 1.3 %copy.14 = bf16[8,1024]{1,0:T(8,128)(2,1)} copy(bf16[8,1024]{1,0:T(8,128)(2,1)} %get-tuple-element.6) | data formatting | bytes 32768
  125.5 0.0 copy-done.1
  125.5 0.0 copy-start
  125.5 0.6 copy.15
  126.1 0.1 copy-done
  126.2 0.6 copy.16
Async XLA Ops:
  124.1 1.3 %copy-start.1 = (bf16[8,1024]{1,0:T(8,128)(2,1)S(1)}, bf16[8,1024]{1,0:T(8,128)(2,1)}, u32[]{:S(2)}) copy-start(bf16[8,1024]{1,0:T(8,128)(2,1)} %get-tuple-element.7) | copy-start | bytes 49156
  125.5 0.7 copy-start

commit v3 on v2

--- a/solution.py
+++ b/solution.py
@@ -12,6 +12,7 @@
 BF16 = jnp.bfloat16
 
 ROWS = 8
+XS = 4
 YS, ZS = 4, 16
 COLS = YS * ZS
 TOK = 8
@@ -80,6 +81,8 @@
     spread,
     rows_in,
     part,
+    pair,
+    pair_got,
     part_got,
     hidden,
     pre,
@@ -103,6 +106,8 @@
     yf_recv_sem,
     a2a_send_sem,
     a2a_recv_sem,
+    pair_send_sem,
+    pair_recv_sem,
     rs_send_sem,
     rs_recv_sem,
     ag_send_sem,
@@ -324,7 +329,7 @@
     def sum_rows(n, dst):
         take("sum", n)
         total = dst[0].astype(F32)
-        for i in range(1, ROWS):
+        for i in range(1, dst.shape[0]):
             total = total + dst[i].astype(F32)
         return total
 
@@ -345,9 +350,34 @@
         @pl.loop(0, 2 * PAD // TILE)
         def _(i):
             cols = pl.ds(pl.multiple_of(i * TILE, TILE), TILE)
-            part[n, :, cols] = dot(rows_in[...], wide[:, cols]).astype(BF16)
-
-        send_rows(n, part.at[n], part_got.at[n])
+            value = dot(rows_in[...], wide[:, cols]).reshape(XS, 2, MINE, TILE)
+            part[n, :, :, :, cols] = value.astype(BF16)
+
+        other = part.at[n, :, 1 - core]
+        got = pair_got.at[n]
+        send(other, got, pair_send_sem.at[n], pair_recv_sem.at[n], x * 2 + 1 - core, c).start()
+        owe(("pair", n), (got, pair_recv_sem.at[n]), (got, pair_send_sem.at[n]))
+
+    def combine(n):
+        take("pair", n)
+        pair[n] = (part[n, :, core].astype(F32) + pair_got[n].astype(F32)).astype(BF16)
+        for o in (2, 1, 3):
+            to = lax.rem(x + o, XS)
+            send(
+                pair.at[n, to],
+                part_got.at[n, x],
+                rs_send_sem.at[n],
+                rs_recv_sem.at[n],
+                to * 2 + core,
+                c,
+            ).start()
+        part_got[n, x] = pair[n, x]
+        most = pl.ds(0, XS - 1)
+        owe(
+            ("sum", n),
+            (part_got.at[n, most], rs_recv_sem.at[n]),
+            (pair.at[n, most], rs_send_sem.at[n]),
+        )
 
     def load_teacher(n):
         group = lax.rem(y + Y_OFFSETS[n], YS)
@@ -416,15 +446,25 @@
         back_send[...] = spread[...].astype(BF16)
         all_to_all(1, back_send, back_got)
 
-    for n in range(YS):
-        load_teacher(n)
-        project(n)
+    load_teacher(0)
+    project(0)
+    load_teacher(1)
+    project(1)
+    combine(0)
+    load_teacher(2)
+    project(2)
+    combine(1)
+    load_teacher(3)
+    project(3)
+    combine(2)
     activate(0)
+    combine(3)
     activate(1)
     take("slots", 0)
     load_slots(got_slots)
     project(STUDENT)
     activate(2)
+    combine(STUDENT)
     activate(3)
     produce_teacher(1)
     produce_teacher(2)
@@ -534,8 +574,10 @@
             pltpu.VMEM((SLOT_ROWS, LANES), BF16),
             pltpu.VMEM((SLOT_ROWS, LANES), F32),
             pltpu.VMEM((CHUNK, WIDTH), BF16),
-            pltpu.VMEM((YS + 1, CHUNK, 2 * PAD), BF16),
-            pltpu.VMEM((YS + 1, ROWS, MINE, 2 * PAD), BF16),
+            pltpu.VMEM((YS + 1, XS, 2, MINE, 2 * PAD), BF16),
+            pltpu.VMEM((YS + 1, XS, MINE, 2 * PAD), BF16),
+            pltpu.VMEM((YS + 1, XS, MINE, 2 * PAD), BF16),
+            pltpu.VMEM((YS + 1, XS, MINE, 2 * PAD), BF16),
             pltpu.VMEM((YS + 1, CHUNK, PAD), BF16),
             pltpu.VMEM((MINE, 2 * PAD), F32),
             pltpu.VMEM((ZS, BLOCK, LANES), F32),
@@ -558,6 +600,8 @@
             sems((YS,)),
             sems((4,)),
             sems((4,)),
+            sems((YS + 1,)),
+            sems((YS + 1,)),
             sems((YS + 2,)),
             sems((YS + 2,)),
             sems((YS + 2,)),

time: 127 us -> 125 us (0.984)
  Pallas kernels: 123 us -> 121 us
    pallas_call x1, Pallas kernels: 123 us -> 121 us  [shards(): pl.pallas_call(kernel, out_shape=(out, out, out), in_specs=[hbm] * 8, out...]
where the time goes in v3:
time: 125 us; the launch traced here: 124 us
  Pallas kernels  121 us (97%)
  local copies, waits for them, and re-layouts  2.66 us (2%)
    pallas_call x1, Pallas kernels, shards(): pl.pallas_call(kernel, out_shape=(out, out, out), in_specs=[hbm] * 8, out...  121 us
    unnamed x7, local copies, waits for them, and re-layouts  2.66 us

profile of v3, /device:TPU:1, one launch (start us, length us, event | category | flops | bytes accessed | tf_op | source)
XLA Modules:
  0.0 124.4 jit_solution(9693183253940324435)
XLA Ops:
  0.6 121.1 %shard_map.103 = (bf16[8,1024]{1,0:T(8,128)(2,1)}, bf16[8,1024]{1,0:T(8,128)(2,1)}, bf16[8,1024]{1,0:T(8,128)(2,1)}) custom-call(bf16[8,1024]{1,0:T(8,128)(2,1)} %teacher_hbm.1, bf16[8,1024]{1,0:T(8,128)(2,1)} %student_hbm.1, bf16[462,1024]{1,0:T(8,128)(2,1)} %bitcast.2, bf16[462,1024]{1,0:T(8,128)(2,1)} %bitcast.3, bf16[462,1024]{1,0:T(8,128)(2,1)} %down_hbm.1, ...), custom_call_target="tpu_custom_call" | custom-call | tf_op jit(solution)/shard_map/pallas_call | solution.py:549
  121.7 0.0 copy-start.1
  121.7 1.3 %copy.14 = bf16[8,1024]{1,0:T(8,128)(2,1)} copy(bf16[8,1024]{1,0:T(8,128)(2,1)} %get-tuple-element.6) | data formatting | bytes 32768
  123.0 0.0 copy-done.1
  123.1 0.0 copy-start
  123.1 0.6 copy.15
  123.7 0.1 copy-done
  123.8 0.6 copy.16
Async XLA Ops:
  121.7 1.3 %copy-start.1 = (bf16[8,1024]{1,0:T(8,128)(2,1)S(1)}, bf16[8,1024]{1,0:T(8,128)(2,1)}, u32[]{:S(2)}) copy-start(bf16[8,1024]{1,0:T(8,128)(2,1)} %get-tuple-element.7) | copy-start | bytes 49156
  123.1 0.7 copy-start

commit v4 on v3

--- a/solution.py
+++ b/solution.py
@@ -31,6 +31,8 @@
 SLOT_ROWS = COLS * MSG
 STUDENT = YS
 Y_OFFSETS = (0, 1, 3, 2)
+HALVES = ((1, 3), (2, 0))
+LINE = ZS * MSG
 TILE = 256
 
 
@@ -95,6 +97,7 @@
     back_got,
     loss_send,
     loss_got,
+    grad_in,
     hid_part,
     hid_got,
     grads,
@@ -305,26 +308,48 @@
         owed["tokens", n] = functools.partial(wait_for, block, yf_recv_sem.at[Y_OFFSETS[n]])
 
 
+    def group_rows(h, i):
+        return pl.multiple_of(lax.rem(y + HALVES[h][i], YS) * LINE, LINE)
+
+    def exchange_half(n, h, src, dst):
+        count = 2 * ZS - h
+
+        @pl.loop(0, count)
+        def _(m):
+            to = lax.rem(y + 1 + h + 2 * lax.rem(m, 2), YS) * ZS + far_first(m // 2)
+            send(
+                src.at[pl.ds(pl.multiple_of(to * MSG, MSG), MSG)],
+                dst.at[pl.ds(pl.multiple_of(c * MSG, MSG), MSG)],
+                a2a_send_sem.at[n],
+                a2a_recv_sem.at[n],
+                r,
+                to,
+            ).start()
+
+        if h == 1:
+            own = pl.ds(pl.multiple_of(c * MSG, MSG), MSG)
+            dst[own, :] = src[own, :]
+        most = pl.ds(0, count * MSG)
+        owe(("slots", n), (dst.at[most], a2a_recv_sem.at[n]), (src.at[most], a2a_send_sem.at[n]))
+
+    def half_rows(h, j):
+        parts = [spread[pl.ds(group_rows(h, i) + j, LINE // SUB, stride=SUB), :] for i in range(2)]
+        return jnp.concatenate(parts, axis=0)
+
+    def store_half(h, j, value):
+        for i in range(2):
+            rows = pl.ds(group_rows(h, i) + j, LINE // SUB, stride=SUB)
+            spread[rows, :] = value[i * (LINE // SUB) : (i + 1) * (LINE // SUB), :]
+
     def send_rows(n, src, dst):
         @pl.loop(0, ROWS - 1)
         def _(m):
             to = row_peer(m)
-            send(
-                src.at[pl.ds(pl.multiple_of(to * MINE, MINE), MINE)],
-                dst.at[r],
-                rs_send_sem.at[n],
-                rs_recv_sem.at[n],
-                to,
-                c,
-            ).start()
-
-        dst[r] = src[pl.ds(pl.multiple_of(r * MINE, MINE), MINE), :]
-        leave = src.at[pl.ds(0, (ROWS - 1) * MINE)]
-        owe(
-            ("sum", n),
-            (dst.at[pl.ds(0, ROWS - 1)], rs_recv_sem.at[n]),
-            (leave, rs_send_sem.at[n]),
-        )
+            send(src.at[to], dst.at[r], rs_send_sem.at[n], rs_recv_sem.at[n], to, c).start()
+
+        dst[r] = src[r]
+        most = pl.ds(0, ROWS - 1)
+        owe(("sum", n), (dst.at[most], rs_recv_sem.at[n]), (src.at[most], rs_send_sem.at[n]))
 
     def sum_rows(n, dst):
         take("sum", n)
@@ -392,9 +417,10 @@
     def load_slots(got):
         spread[...] = got[...].astype(F32)
         for j in range(SUB):
-            rows_in[:, j * LANES : (j + 1) * LANES] = spread[
-                pl.ds(j, SLOTS, stride=SUB), :
-            ].astype(BF16)
+            halves = [half_rows(h, j).reshape(ROWS, SUB, LANES) for h in range(2)]
+            rows_in[:, j * LANES : (j + 1) * LANES] = (
+                jnp.concatenate(halves, axis=1).reshape(SLOTS, LANES).astype(BF16)
+            )
 
     def activate(n):
         total = sum_rows(n, part_got.at[n])
@@ -403,9 +429,11 @@
             pre[...] = total
         gather_rows(n, hidden.at[n], (gate / (1.0 + jnp.exp(-gate)) * up).astype(BF16))
 
-    def store_slots(value, cols, first):
+    def store_slots(value, first):
         for j in range(TILE // LANES):
-            spread[pl.ds(first + j, SLOTS, stride=SUB), :] = value[:, j * LANES : (j + 1) * LANES]
+            rows = value[:, j * LANES : (j + 1) * LANES].reshape(ROWS, 2, SUB, LANES)
+            for h in range(2):
+                store_half(h, first + j, rows[:, h].reshape(SLOTS // 2, LANES))
 
     def produce_teacher(n):
         take("gather", n)
@@ -442,7 +470,7 @@
         take("gather", STUDENT)
         for i in range(WIDTH // TILE):
             value = dot(hidden[STUDENT], down[:, i * TILE : (i + 1) * TILE])
-            store_slots(value, i, i * (TILE // LANES))
+            store_slots(value, i * (TILE // LANES))
         back_send[...] = spread[...].astype(BF16)
         all_to_all(1, back_send, back_got)
 
@@ -509,31 +537,75 @@
     student = dot(weighting[...], back_got[...]).astype(BF16).astype(F32)
     loss = (student - teacher).astype(BF16)
     loss_send[...] = dot(weighting_t[...], loss).astype(BF16)
-    all_to_all(2, loss_send, loss_got)
+    for h in range(2):
+        exchange_half(2 + h, h, loss_send, loss_got)
     student_out[...] = from_lane_rows(student).astype(BF16)
-
-    take("slots", 2)
-    load_slots(loss_got)
-
-    for i in range(PAD // TILE):
-        units = slice(i * TILE, (i + 1) * TILE)
-        hid_part[:, units] = dot(rows_in[...], down_t[:, units]).astype(BF16)
-    send_rows(YS + 1, hid_part, hid_got)
     pre_gate, pre_up = pre[:, :PAD], pre[:, PAD:]
     logistic = 1.0 / (1.0 + jnp.exp(-pre_gate))
-    slope = logistic * (1.0 + pre_gate * (1.0 - logistic))
-    hidden_grad = sum_rows(YS + 1, hid_got)
-    gate_grad = hidden_grad * pre_up * slope
-    up_grad = hidden_grad * (pre_gate * logistic)
-    both = jnp.concatenate([gate_grad, up_grad], axis=1).astype(BF16)
-    gather_rows(YS + 1, grads, both)
-    take("gather", YS + 1)
-    for i in range(WIDTH // TILE):
-        value = dot(grads[...], wide_t[:, i * TILE : (i + 1) * TILE])
-        store_slots(value, i, i * (TILE // LANES))
-    last_send[...] = spread[...].astype(BF16)
-    all_to_all(3, last_send, last_got)
-    take("slots", 3)
+    pre[:, PAD:] = pre_up * (logistic * (1.0 + pre_gate * (1.0 - logistic)))
+    pre[:, :PAD] = pre_gate * logistic
+
+    def hidden_half(h):
+        take("slots", 2 + h)
+        for i in range(2):
+            rows = pl.ds(group_rows(h, i), LINE)
+            spread[rows, :] = loss_got[rows, :].astype(F32)
+        for j in range(SUB):
+            grad_in[:, j * LANES : (j + 1) * LANES] = half_rows(h, j).astype(BF16)
+        for i in range(PAD // TILE):
+            value = dot(grad_in[...], down_t[:, i * TILE : (i + 1) * TILE])
+            parts = [
+                value[:, j * LANES : (j + 1) * LANES].reshape(ROWS, SUB, LANES)
+                for j in range(TILE // LANES)
+            ]
+            rows = slice(i * 2 * SUB, (i + 1) * 2 * SUB)
+            hid_part[h, :, rows, :] = jnp.concatenate(parts, axis=1).astype(BF16)
+        send_rows(YS + 1 + h, hid_part.at[h], hid_got.at[h])
+
+    def grads_half(h):
+        n = YS + 1 + h
+        total = sum_rows(n, hid_got.at[h])
+        parts = [total[j * SUB : (j + 1) * SUB, :] for j in range(PAD // LANES)]
+        hidden_grad = jnp.concatenate(parts, axis=1)
+        mine = slice(h * SUB, (h + 1) * SUB)
+        gate_grad = hidden_grad * pre[mine, PAD:]
+        up_grad = hidden_grad * pre[mine, :PAD]
+        both = jnp.concatenate([gate_grad, up_grad], axis=1)
+        grads[h, r] = to_lane_rows(both).astype(BF16)
+
+        @pl.loop(0, ROWS - 1)
+        def _(m):
+            block = grads.at[h, r]
+            send(block, block, ag_send_sem.at[n], ag_recv_sem.at[n], row_peer(m), c).start()
+
+        most = grads.at[h, pl.ds(0, ROWS - 1)]
+        owe(("gather", n), (most, ag_recv_sem.at[n]), (most, ag_send_sem.at[n]))
+
+    def rows_half(h):
+        take("gather", YS + 1 + h)
+        blocks = grads[h].astype(F32).reshape(ROWS, SUB, SUB, LANES)
+        for j in range(SUB):
+            grad_in[:, j * LANES : (j + 1) * LANES] = (
+                blocks[:, j].reshape(SLOTS // 2, LANES).astype(BF16)
+            )
+        for i in range(WIDTH // TILE):
+            value = dot(grad_in[...], wide_t[:, i * TILE : (i + 1) * TILE])
+            for j in range(TILE // LANES):
+                at = i * (TILE // LANES) + j
+                store_half(h, at, value[:, j * LANES : (j + 1) * LANES])
+        for i in range(2):
+            rows = pl.ds(group_rows(h, i), LINE)
+            last_send[rows, :] = spread[rows, :].astype(BF16)
+        exchange_half(4 + h, h, last_send, last_got)
+
+    hidden_half(0)
+    grads_half(0)
+    hidden_half(1)
+    rows_half(0)
+    grads_half(1)
+    rows_half(1)
+    take("slots", 4)
+    take("slots", 5)
     grad = dot(placing[...], last_got[...])
     input_grad[...] = from_lane_rows(grad).astype(BF16)
 
@@ -589,23 +661,24 @@
             pltpu.VMEM((SLOT_ROWS, LANES), BF16),
             pltpu.VMEM((SLOT_ROWS, LANES), BF16),
             pltpu.VMEM((SLOT_ROWS, LANES), BF16),
-            pltpu.VMEM((CHUNK, PAD), BF16),
-            pltpu.VMEM((ROWS, MINE, PAD), BF16),
-            pltpu.VMEM((CHUNK, 2 * PAD), BF16),
+            pltpu.VMEM((SLOTS // 2, WIDTH), BF16),
+            pltpu.VMEM((2, ROWS, PAD // LANES * SUB, LANES), BF16),
+            pltpu.VMEM((2, ROWS, PAD // LANES * SUB, LANES), BF16),
+            pltpu.VMEM((2, ROWS, 2 * PAD // LANES * SUB, LANES), BF16),
             pltpu.VMEM((SLOT_ROWS, LANES), BF16),
             pltpu.VMEM((SLOT_ROWS, LANES), BF16),
             sems,
             sems((ZS,)),
             sems,
             sems((YS,)),
-            sems((4,)),
-            sems((4,)),
+            sems((6,)),
+            sems((6,)),
             sems((YS + 1,)),
             sems((YS + 1,)),
-            sems((YS + 2,)),
-            sems((YS + 2,)),
-            sems((YS + 2,)),
-            sems((YS + 2,)),
+            sems((YS + 3,)),
+            sems((YS + 3,)),
+            sems((YS + 3,)),
+            sems((YS + 3,)),
             sems,
             sems((ZS,)),
             sems,

time: 125 us -> 121 us (0.968)
  Pallas kernels: 121 us -> 117 us
    pallas_call x1, Pallas kernels: 121 us -> 117 us  [shards(): pl.pallas_call(kernel, out_shape=(out, out, out), in_specs=[hbm] * 8, out...]
where the time goes in v4:
time: 121 us; the launch traced here: 120 us
  Pallas kernels  117 us (97%)
  local copies, waits for them, and re-layouts  2.66 us (2%)
    pallas_call x1, Pallas kernels, shards(): pl.pallas_call(kernel, out_shape=(out, out, out), in_specs=[hbm] * 8, out...  117 us
    unnamed x7, local copies, waits for them, and re-layouts  2.66 us

profile of v4, /device:TPU:1, one launch (start us, length us, event | category | flops | bytes accessed | tf_op | source)
XLA Modules:
  0.0 120.0 jit_solution(2036131304483289096)
XLA Ops:
  0.6 116.7 %shard_map.103 = (bf16[8,1024]{1,0:T(8,128)(2,1)}, bf16[8,1024]{1,0:T(8,128)(2,1)}, bf16[8,1024]{1,0:T(8,128)(2,1)}) custom-call(bf16[8,1024]{1,0:T(8,128)(2,1)} %teacher_hbm.1, bf16[8,1024]{1,0:T(8,128)(2,1)} %student_hbm.1, bf16[462,1024]{1,0:T(8,128)(2,1)} %bitcast.2, bf16[462,1024]{1,0:T(8,128)(2,1)} %bitcast.3, bf16[462,1024]{1,0:T(8,128)(2,1)} %down_hbm.1, ...), custom_call_target="tpu_custom_call" | custom-call | tf_op jit(solution)/shard_map/pallas_call | solution.py:621
  117.3 0.0 copy-start.1
  117.4 1.3 %copy.14 = bf16[8,1024]{1,0:T(8,128)(2,1)} copy(bf16[8,1024]{1,0:T(8,128)(2,1)} %get-tuple-element.6) | data formatting | bytes 32768
  118.7 0.0 copy-done.1
  118.7 0.0 copy-start
  118.7 0.6 copy.15
  119.3 0.1 copy-done
  119.4 0.6 copy.16
Async XLA Ops:
  117.3 1.3 %copy-start.1 = (bf16[8,1024]{1,0:T(8,128)(2,1)S(1)}, bf16[8,1024]{1,0:T(8,128)(2,1)}, u32[]{:S(2)}) copy-start(bf16[8,1024]{1,0:T(8,128)(2,1)} %get-tuple-element.7) | copy-start | bytes 49156
  118.7 0.7 copy-start

commit v5 on v4

--- a/solution.py
+++ b/solution.py
@@ -30,7 +30,7 @@
 MSG = CAP * SUB
 SLOT_ROWS = COLS * MSG
 STUDENT = YS
-Y_OFFSETS = (0, 1, 3, 2)
+Y_OFFSETS = (0, 2, 1, 3)
 HALVES = ((1, 3), (2, 0))
 LINE = ZS * MSG
 TILE = 256

time: 121 us -> 121 us (level)
  no operation moved by 1% of the time
where the time goes in v5:
time: 121 us
  Pallas kernels  118 us (98%)
  local copies, waits for them, and re-layouts  2.66 us (2%)
    pallas_call x1, Pallas kernels, shards(): pl.pallas_call(kernel, out_shape=(out, out, out), in_specs=[hbm] * 8, out...  118 us
    unnamed x7, local copies, waits for them, and re-layouts  2.66 us

profile of v5, /device:TPU:1, one launch (start us, length us, event | category | flops | bytes accessed | tf_op | source)
XLA Modules:
  0.0 120.8 jit_solution(4120335932365464323)
XLA Ops:
  0.6 117.5 %shard_map.103 = (bf16[8,1024]{1,0:T(8,128)(2,1)}, bf16[8,1024]{1,0:T(8,128)(2,1)}, bf16[8,1024]{1,0:T(8,128)(2,1)}) custom-call(bf16[8,1024]{1,0:T(8,128)(2,1)} %teacher_hbm.1, bf16[8,1024]{1,0:T(8,128)(2,1)} %student_hbm.1, bf16[462,1024]{1,0:T(8,128)(2,1)} %bitcast.2, bf16[462,1024]{1,0:T(8,128)(2,1)} %bitcast.3, bf16[462,1024]{1,0:T(8,128)(2,1)} %down_hbm.1, ...), custom_call_target="tpu_custom_call" | custom-call | tf_op jit(solution)/shard_map/pallas_call | solution.py:621
  118.2 0.0 copy-start.1
  118.2 1.3 %copy.14 = bf16[8,1024]{1,0:T(8,128)(2,1)} copy(bf16[8,1024]{1,0:T(8,128)(2,1)} %get-tuple-element.6) | data formatting | bytes 32768
  119.5 0.0 copy-done.1
  119.5 0.0 copy-start
  119.5 0.6 copy.15
  120.1 0.1 copy-done
  120.2 0.6 copy.16
Async XLA Ops:
  118.2 1.3 %copy-start.1 = (bf16[8,1024]{1,0:T(8,128)(2,1)S(1)}, bf16[8,1024]{1,0:T(8,128)(2,1)}, u32[]{:S(2)}) copy-start(bf16[8,1024]{1,0:T(8,128)(2,1)} %get-tuple-element.7) | copy-start | bytes 49156
  119.5 0.7 copy-start
